TPU v7x, 512 devices: a whole 4x8x8 slice. The times are simulated.
512 devices in a mesh: ctx: 16 (over x, z_hi), dp: 8 (over y), tp: 4 (over z_lo, core).
Axes of the slice: x: 4, y: 8, z: 8 (z_hi: 4, z_lo: 2; z = z_hi * 2 + z_lo), core: 2. Of those that a mesh axis runs over, the one named last changes fastest.
Arguments:
- token_ids: int32 [4, 16], replicated, may hold values from 0 to 50279
- decode_prompt: int32 [16], replicated, may hold values from 0 to 15, as said below
- embedding: bfloat16 [50280, 4096], P('dp', ('ctx', 'tp')), may hold values from -6 to 6
- norm_gain: float32 [4096], replicated, may hold values from 0.1 to 1.9
- w_zx: bfloat16 [2, 128, 64, 4096], P(None, ('tp', 'ctx')), may hold values from -0.09375 to 0.09375
- w_bcdt: bfloat16 [4096, 384], P(None, ('ctx', 'tp')), may hold values from -0.09375 to 0.09375
- conv_x_weight: float32 [4, 128, 64], P(None, ('tp', 'ctx')), may hold values from -3 to 3
- conv_x_bias: float32 [128, 64], P(('tp', 'ctx')), may hold values from -3 to 3
- conv_bc_weight: float32 [4, 256], replicated, may hold values from -3 to 3
- conv_bc_bias: float32 [256], replicated, may hold values from -3 to 3
- dt_bias: float32 [128], P(('tp', 'ctx')), may hold values from -4 to -1
- a_log: float32 [128], P(('tp', 'ctx')), may hold values from 0 to 2.7
- d_skip: float32 [128], P(('tp', 'ctx')), may hold values from 0.5 to 1.5
- gate_norm_gain: float32 [128, 64], P(('tp', 'ctx')), may hold values from 0.1 to 1.9
- w_out: bfloat16 [128, 64, 4096], P(('tp', 'ctx')), may hold values from -0.0625 to 0.0625
- state_parts: bfloat16 [16, 16, 128, 64, 128], P('ctx', 'dp', 'tp'), may hold values from -6 to 6
- seg_rate: float32 [16, 16, 128], P('ctx', 'dp', 'tp'), may hold values from 0 to 2
- x_tail: bfloat16 [16, 3, 128, 64], P('dp', None, ('tp', 'ctx')), may hold values from -6 to 6
- bc_tail: bfloat16 [16, 3, 256], P('dp'), may hold values from -6 to 6
Outputs:
- mixer_out: bfloat16 [4, 16, 4096], P(None, 'dp', ('ctx', 'tp'))
- final_state: float32 [16, 128, 64, 128], P('dp', ('tp', 'ctx'))
Inputs may be any that keep to these rules, and one draw needn't show every extreme that they name: decode_prompt is a permutation of the prompts; slot s is decoded by dp group s // 2, and prompt q is held by dp group q // 2; the 2 prompts held by one dp group are decoded by 2 different dp groups.
All inputs are finite; a program needn't handle non-finite values.
Results may differ from a plain program's by a relative error of at most 0.02.
Values may be sent and summed in bfloat16 or wider, within the bound.
No kernel may reach another device: no remote copies, remote signals or barrier semaphores. Data moves between devices by JAX's collectives and lax.ppermute only.
A program may use at most 64 MiB of HBM per device.

v0:
```python
import jax
import jax.numpy as jnp
from jax import lax
from jax.sharding import PartitionSpec as P

HEADS = 128
HEAD_DIM = 64
epsilon = 1e-05


def from_everyone(shard, axis):
    count = lax.axis_size(axis)
    return lax.all_to_all(
        jnp.broadcast_to(shard[None], (count, *shard.shape)), axis, 0, 0, tiled=True
    )


def folded_in_pairs(pieces, combine):
    while len(jax.tree.leaves(pieces)[0]) > 1:
        pieces = jax.vmap(combine)(*(pieces[side::2] for side in (0, 1)))
    return pieces[0]


def prefix(shard, axis, combine, identity):
    count, here = (lax.axis_size(axis), lax.axis_index(axis))
    passed = jnp.arange(count) > here

    def kept(part, zero, own):
        part = jnp.where(
            passed.reshape(-1, *(1 for _ in own.shape)), part, jnp.asarray(zero, own.dtype)
        )
        return part[::-1]

    pieces = from_everyone(shard, axis)
    return folded_in_pairs(kept(pieces, identity, shard), combine)


def split_up(shard, dim, count):
    before, after = (shard.shape[:dim], shard.shape[dim + 1 :])
    return jnp.moveaxis(shard.reshape(*before, count, -1, *after), dim, 0)


def sum_at_owner(shard, axis, dim):
    count = lax.axis_size(axis)
    pieces = lax.all_to_all(split_up(shard, dim, count), axis, 0, 0, tiled=True)
    return jnp.sum(pieces.astype(jnp.float32), axis=0)


def rows_first(arrays, axis, dims):
    turned = [jnp.moveaxis(a, dim, 0) for a, dim in zip(arrays, dims)]
    widths = [t[0].size for t in turned]
    both = jnp.concatenate([t.reshape(-1, w) for t, w in zip(turned, widths)], axis=1)
    filled = lax.all_gather(both, axis, axis=0, tiled=True)
    pieces = jnp.split(filled, [sum(widths[:k]) for k in range(1, len(widths))], axis=1)
    return tuple(
        (
            jnp.moveaxis(b.reshape(-1, *t.shape[1:]), 0, dim)
            for b, t, dim in zip(pieces, turned, dims)
        )
    )


def laid_out(pieces, dim):
    dims = list(pieces.shape[1:])
    dims[dim] *= pieces.shape[0]
    return jnp.moveaxis(pieces, 0, dim).reshape(dims)


def collect(shard, axis, dim):
    pieces = from_everyone(shard, axis)
    return laid_out(pieces, dim)


def over_copies(shard, axis):
    everything = from_everyone(shard, axis)
    return jnp.sum(everything, axis=0)


def sum_at_owner_2(shard, axis, dim):
    pieces = split_up(shard, dim, lax.axis_size(axis))
    arrived = lax.all_to_all(pieces, axis, split_axis=0, concat_axis=0, tiled=True)
    return arrived.sum(axis=0)


def rms_scale(values, gain):
    return values * lax.rsqrt(jnp.mean(values * values, axis=-1, keepdims=True) + epsilon) * gain


def select_rows(picker, values):
    return jnp.tensordot(picker, values, axes=1, precision=lax.Precision.HIGHEST)


def add_rates(earlier, later_one):
    return earlier + later_one


def per_device(
    token_ids,
    decode_prompt,
    embedding,
    norm_gain,
    w_zx,
    w_bcdt,
    conv_x_weight,
    conv_x_bias,
    conv_bc_weight,
    conv_bc_bias,
    dt_bias,
    a_log,
    d_skip,
    gate_norm_gain,
    w_out,
    state_parts,
    seg_rate,
    x_tail,
    bc_tail,
):
    group = lax.axis_index("dp")
    local_count = state_parts.shape[1]
    slot_count = decode_prompt.shape[0]
    head_count = w_zx.shape[1]
    state_width = conv_bc_bias.shape[0] // 2
    after_rates = prefix(seg_rate, "ctx", add_rates, jnp.zeros_like(seg_rate))
    seg_weight = jnp.exp(-after_rates[0])
    scaled = seg_weight[:, :, None, None] * state_parts[0].astype(jnp.float32)
    combined = sum_at_owner(scaled.astype(jnp.bfloat16), "ctx", 1)
    tails_x = x_tail.astype(jnp.float32)
    tails_bc = bc_tail.astype(jnp.float32)
    own_slots = lax.dynamic_slice_in_dim(decode_prompt, group * local_count, local_count)
    prompt_ids = jnp.arange(slot_count, dtype=jnp.int32)
    every_state, every_x, every_bc = tuple(
        (
            part.astype(jnp.float32)
            for part in rows_first(
                (
                    combined.astype(jnp.bfloat16),
                    tails_x.astype(jnp.bfloat16),
                    tails_bc.astype(jnp.bfloat16),
                ),
                "dp",
                (0, 0, 0),
            )
        )
    )
    picker = (own_slots[:, None] == prompt_ids[None, :]).astype(jnp.float32)
    ssm_state = select_rows(picker, every_state)
    x_window = select_rows(picker, every_x)
    bc_window = select_rows(picker, every_bc)
    vocab_rows = embedding.shape[0]
    holder = (decode_prompt[:, None] == prompt_ids[None, :]).astype(jnp.int32)
    slot_tokens = jnp.sum(token_ids[:, None, :] * holder[None], axis=2)
    offset_tokens = slot_tokens - group * vocab_rows
    inside = (offset_tokens >= 0) & (offset_tokens < vocab_rows)
    looked = jnp.take(embedding, jnp.clip(offset_tokens, 0, vocab_rows - 1), axis=0)
    partial_rows = jnp.where(inside[..., None], looked.astype(jnp.float32), 0.0)
    own_rows = sum_at_owner(partial_rows.astype(jnp.bfloat16), "dp", 1)
    embedded = collect(own_rows.astype(jnp.bfloat16), ("ctx", "tp"), 2)
    steps_count = embedded.shape[0]
    flat_rows = embedded.reshape(-1, embedded.shape[2]).astype(jnp.float32)
    normed = rms_scale(flat_rows, norm_gain).astype(jnp.bfloat16)
    projected = jnp.einsum("rd,khed->krhe", normed, w_zx, preferred_element_type=jnp.float32)
    projected = projected.reshape(
        2, steps_count, local_count, projected.shape[2], projected.shape[3]
    )
    columns = collect(jnp.dot(normed, w_bcdt, preferred_element_type=jnp.float32), ("ctx", "tp"), 1)
    columns = columns.reshape(steps_count, local_count, -1)
    head_block = lax.axis_index("tp") * lax.axis_size("ctx") + lax.axis_index("ctx")
    head_start = 2 * state_width + head_block * head_count
    dt_raw = lax.dynamic_slice_in_dim(columns, head_start, head_count, 2)
    decay_rate = -jnp.exp(a_log)
    gated_steps = []
    for moment in range(steps_count):
        x_window = jnp.concatenate([x_window, projected[1, moment][:, None]], axis=1)
        bc_window = jnp.concatenate(
            [bc_window, columns[moment, :, None, : 2 * state_width]], axis=1
        )
        x_conv = jax.nn.silu(jnp.einsum("pkhe,khe->phe", x_window, conv_x_weight) + conv_x_bias)
        bc_conv = jax.nn.silu(jnp.einsum("pkn,kn->pn", bc_window, conv_bc_weight) + conv_bc_bias)
        step_size = jax.nn.softplus(dt_raw[moment] + dt_bias)
        retain = jnp.exp(step_size * decay_rate)
        ssm_state = (
            retain[:, :, None, None] * ssm_state
            + (step_size[:, :, None] * x_conv)[:, :, :, None] * bc_conv[:, None, None, :state_width]
        )
        output = (
            jnp.einsum("phen,pn->phe", ssm_state, bc_conv[:, state_width:])
            + d_skip[None, :, None] * x_conv
        )
        gated_steps.append(output * jax.nn.silu(projected[0, moment]))
        x_window = x_window[:, 1:]
        bc_window = bc_window[:, 1:]
    gated_all = jnp.stack(gated_steps)
    local_squares = jnp.sum(gated_all * gated_all, axis=(2, 3))
    total_squares = over_copies(local_squares, ("ctx", "tp"))
    inverse = lax.rsqrt(total_squares / (HEADS * HEAD_DIM) + epsilon)
    normed_out = (gated_all * inverse[:, :, None, None] * gate_norm_gain).astype(jnp.bfloat16)
    partial_out = jnp.einsum("tphe,hed->tpd", normed_out, w_out, preferred_element_type=jnp.float32)
    mixed = sum_at_owner_2(partial_out, ("ctx", "tp"), 2)
    return (mixed.astype(jnp.bfloat16), ssm_state)


def solution(mesh):
    return jax.shard_map(
        per_device,
        mesh=mesh,
        in_specs=(
            P(),
            P(),
            P("dp", ("ctx", "tp")),
            P(),
            P(None, ("tp", "ctx"), None, None),
            P(None, ("ctx", "tp")),
            P(None, ("tp", "ctx"), None),
            P(("tp", "ctx"), None),
            P(),
            P(),
            P(("tp", "ctx")),
            P(("tp", "ctx")),
            P(("tp", "ctx")),
            P(("tp", "ctx"), None),
            P(("tp", "ctx"), None, None),
            P("ctx", "dp", "tp", None, None),
            P("ctx", "dp", "tp"),
            P("dp", None, ("tp", "ctx"), None),
            P("dp", None, None),
        ),
        out_specs=(P(None, "dp", ("ctx", "tp")), P("dp", ("tp", "ctx"), None, None)),
        check_vma=False,
    )
```

profile of v0, /device:TPU:1, one launch (start us, length us, event | category | flops | bytes accessed | tf_op | source)
XLA Modules:
  0.0 178.2 jit_solution(10364687955391233364)
XLA Ops:
  0.6 1.4 broadcast_in_dim.52
  2.1 13.4 %all-to-all-start.3 = ((f32[16,1,2,32]{3,2,1,0:T(2,128)}), f32[16,1,2,32]{3,2,1,0:T(2,128)S(1)}, u32[]{:S(2)}, u32[]{:S(2)}) async-start(f32[16,1,2,32]{3,2,1,0:T(2,128)} %broadcast_in_dim.52), calls=%async_computation.3 | async-start | bytes 32768 | tf_op jit(solution)/shard_map/all_to_all | solution.py:13
  15.5 0.7 fusion.42
  16.2 0.8 multiply_reduce_fusion
  17.2 0.1 copy.221
  17.5 2.6 %copy.222 = bf16[6285,64]{1,0:T(8,128)(2,1)} copy(bf16[6285,64]{0,1:T(8,128)(2,1)} %param.21) | data formatting | bytes 1608960 | tf_op args[2]
  20.1 2.2 %gather_fusion = bf16[64,64]{1,0:T(8,128)(2,1)S(1)} fusion(bf16[6285,64]{1,0:T(8,128)(2,1)} %copy.222, s32[1024]{0:T(1024)S(1)} %pad_clamp_fusion), kind=kCustom, calls=%fused_computation | custom fusion | bytes 16640 | tf_op jit(solution)/shard_map/jit(_take)/gather | solution.py:154
  22.4 0.1 fusion.19
  22.5 0.7 reshape.439
  23.2 1.1 all-to-all-done.3
  24.3 6.8 %all-to-all-start = ((bf16[8,2,256]{2,1,0:T(2,128)(2,1)}), bf16[8,2,256]{2,1,0:T(2,128)(2,1)S(1)}, u32[]{:S(2)}, u32[]{:S(2)}) async-start(bf16[8,2,256]{2,1,0:T(2,128)(2,1)} %reshape.439), calls=%async_computation | async-start | bytes 16384 | tf_op jit(solution)/shard_map/all_to_all | solution.py:45
  31.3 6.4 %all-to-all-done = bf16[8,2,256]{2,1,0:T(2,128)(2,1)S(1)} async-done(((bf16[8,2,256]{2,1,0:T(2,128)(2,1)}), bf16[8,2,256]{2,1,0:T(2,128)(2,1)S(1)}, u32[]{:S(2)}, u32[]{:S(2)}) %all-to-all-start) | async-done | bytes 8224 | tf_op jit(solution)/shard_map/all_to_all | solution.py:45
  38.0 0.8 reshape.441
  38.7 11.3 %all-to-all-start.1 = ((bf16[64,2,256]{2,1,0:T(2,128)(2,1)}), bf16[64,2,256]{2,1,0:T(2,128)(2,1)S(1)}, u32[]{:S(2)}, u32[]{:S(2)}) async-start(bf16[64,2,256]{2,1,0:T(2,128)(2,1)} %reshape.441), calls=%async_computation.1 | async-start | bytes 131072 | tf_op jit(solution)/shard_map/all_to_all | solution.py:13
  50.2 9.7 %all-to-all-done.1 = bf16[64,2,256]{2,1,0:T(2,128)(2,1)S(1)} async-done(((bf16[64,2,256]{2,1,0:T(2,128)(2,1)}), bf16[64,2,256]{2,1,0:T(2,128)(2,1)S(1)}, u32[]{:S(2)}, u32[]{:S(2)}) %all-to-all-start.1) | async-done | bytes 65568 | tf_op jit(solution)/shard_map/all_to_all | solution.py:13
  59.9 0.1 reshape.442
  60.1 0.3 fusion.5
  60.4 0.1 reshape.396
  60.7 0.2 fusion.86
  60.9 0.8 broadcast_in_dim.49
  61.6 4.4 %all-to-all-start.2 = ((f32[64,8,6]{2,1,0:T(8,128)}), f32[64,8,6]{2,1,0:T(8,128)S(1)}, u32[]{:S(2)}, u32[]{:S(2)}) async-start(f32[64,8,6]{2,1,0:T(8,128)} %broadcast_in_dim.49), calls=%async_computation.2 | async-start | bytes 524288 | tf_op jit(solution)/shard_map/all_to_all | solution.py:13
  66.1 1.5 fusion.2
  67.6 1.1 copy.227
  68.7 9.4 %all-to-all-done.2 = f32[64,8,6]{2,1,0:T(8,128)S(1)} async-done(((f32[64,8,6]{2,1,0:T(8,128)}), f32[64,8,6]{2,1,0:T(8,128)S(1)}, u32[]{:S(2)}, u32[]{:S(2)}) %all-to-all-start.2) | async-done | bytes 12320 | tf_op jit(solution)/shard_map/all_to_all | solution.py:13
  78.1 4.8 %all-to-all-start.4 = ((bf16[16,2,2,64,128]{4,3,2,1,0:T(8,128)(2,1)}), bf16[16,2,2,64,128]{4,3,2,1,0:T(8,128)(2,1)S(1)}, u32[]{:S(2)}, u32[]{:S(2)}) async-start(bf16[16,2,2,64,128]{4,3,2,1,0:T(8,128)(2,1)} %copy.227), calls=%async_computation.4 | async-start | bytes 2097152 | tf_op jit(solution)/shard_map/all_to_all | solution.py:45
  82.9 0.6 reshape.389
  83.6 0.6 dynamic_slice.7
  84.2 0.5 exponential_negate_fusion
  84.7 1.6 fusion.12
  86.3 0.6 slice_bitcast_fusion.3
  86.9 0.8 copy.225
  87.7 1.1 reshape_reshape.4
  88.8 0.8 multiply_exponential_fusion.3
  90.0 0.7 copy.246
  90.7 0.7 copy.241
  91.4 0.6 copy.236
  92.0 0.7 copy.226
  92.7 0.6 slice_bitcast_fusion.5
  93.3 13.3 %all-to-all-done.4 = bf16[16,2,2,64,128]{4,3,2,1,0:T(8,128)(2,1)S(1)} async-done(((bf16[16,2,2,64,128]{4,3,2,1,0:T(8,128)(2,1)}), bf16[16,2,2,64,128]{4,3,2,1,0:T(8,128)(2,1)S(1)}, u32[]{:S(2)}, u32[]{:S(2)}) %all-to-all-start.4) | async-done | bytes 1048608 | tf_op jit(solution)/shard_map/all_to_all | solution.py:45
  106.6 0.2 reduce_sum.72
  106.9 20.3 %all-gather = bf16[8,2,17536]{2,1,0:T(2,128)(2,1)S(1)} all-gather(bf16[1,2,17536]{2,1,0:T(2,128)(2,1)S(1)} %maximum_bitcast_fusion), channel_id=1, replica_groups=mesh['ctx'=16,'dp'=8,'tp'=4] {'dp'}, dimensions={0}, use_global_device_ids=true | all-gather | bytes 631296 | tf_op jit(solution)/shard_map/all_gather | solution.py:53
  127.2 0.2 reshape.409
  127.6 0.2 fusion.17
  127.8 0.2 fusion.14
  128.1 0.6 broadcast_multiply_fusion.3
  128.8 0.1 copy.244
  129.3 0.7 fusion.35
  130.0 0.7 divide_multiply_fusion.10
  130.8 1.7 multiply_add_fusion
  132.5 0.1 fusion.10
  132.7 0.2 fusion.6
  132.8 0.2 fusion.8
  133.0 0.2 fusion.93
  133.5 26.3 %all_to_all.35 = f32[64,4,2]{1,2,0:T(2,128)S(1)} all-to-all(f32[64,4,2]{1,2,0:T(2,128)S(1)} %broadcast_in_dim.54), channel_id=1, replica_groups=mesh['ctx'=16,'dp'=8,'tp'=4] {'ctx','tp'}, dimensions={0} | all-to-all | bytes 4096 | tf_op jit(solution)/shard_map/all_to_all | solution.py:13
  160.0 0.8 multiply_convert_fusion.1
  160.8 0.3 convolution_bitcast_fusion
  161.1 0.2 reshape.395
  161.3 0.2 copy.372
  161.5 0.2 reshape.443
  161.7 14.2 %all_to_all.36 = f32[64,1,512]{2,1,0:T(1,128)S(1)} all-to-all(f32[64,1,512]{2,1,0:T(1,128)S(1)} %reshape.443), channel_id=1, replica_groups=mesh['ctx'=16,'dp'=8,'tp'=4] {'ctx','tp'}, dimensions={0} | all-to-all | bytes 262144 | tf_op jit(solution)/shard_map/all_to_all | solution.py:81
  175.9 0.5 broadcast.320
  176.4 0.9 reduce.20
  177.4 0.2 reshape.444
  177.7 0.6 copy.255
  (95 shorter events, 2.8 us)
Async XLA Ops:
  0.6 84.1 %copy-start = (bf16[2,2,64,4096]{3,2,1,0:T(8,128)(2,1)S(1)}, bf16[2,2,64,4096]{3,2,1,0:T(8,128)(2,1)}, u32[]{:S(2)}) copy-start(bf16[2,2,64,4096]{3,2,1,0:T(8,128)(2,1)} %param.23) | copy-start | bytes 6291460
  2.1 22.3 %all-to-all-start.3 = ((f32[16,1,2,32]{3,2,1,0:T(2,128)}), f32[16,1,2,32]{3,2,1,0:T(2,128)S(1)}, u32[]{:S(2)}, u32[]{:S(2)}) async-start(f32[16,1,2,32]{3,2,1,0:T(2,128)} %broadcast_in_dim.52), calls=%async_computation.3 | async-start | bytes 32768 | tf_op jit(solution)/shard_map/all_to_all | solution.py:13
  17.5 43.2 %copy-start.3 = (f32[4096]{0:T(1024)S(1)}, f32[4096]{0:T(1024)}, u32[]{:S(2)}) copy-start(f32[4096]{0:T(1024)} %param.22) | copy-start | bytes 49156
  17.5 43.2 %copy-start.4 = (bf16[4096,6]{0,1:T(8,128)(2,1)S(1)}, bf16[4096,6]{0,1:T(8,128)(2,1)}, u32[]{:S(2)}) copy-start(bf16[4096,6]{0,1:T(8,128)(2,1)} %param.24) | copy-start | bytes 147460
  24.3 13.4 %all-to-all-start = ((bf16[8,2,256]{2,1,0:T(2,128)(2,1)}), bf16[8,2,256]{2,1,0:T(2,128)(2,1)S(1)}, u32[]{:S(2)}, u32[]{:S(2)}) async-start(bf16[8,2,256]{2,1,0:T(2,128)(2,1)} %reshape.439), calls=%async_computation | async-start | bytes 16384 | tf_op jit(solution)/shard_map/all_to_all | solution.py:45
  38.7 21.1 %all-to-all-start.1 = ((bf16[64,2,256]{2,1,0:T(2,128)(2,1)}), bf16[64,2,256]{2,1,0:T(2,128)(2,1)S(1)}, u32[]{:S(2)}, u32[]{:S(2)}) async-start(bf16[64,2,256]{2,1,0:T(2,128)(2,1)} %reshape.441), calls=%async_computation.1 | async-start | bytes 131072 | tf_op jit(solution)/shard_map/all_to_all | solution.py:13
  60.7 8.1 %copy-start.11 = (f32[8]{0:T(128)}, f32[8]{0:T(128)S(1)}, u32[]{:S(2)}) copy-start(f32[8]{0:T(128)S(1)} %rsqrt.19) | copy-start | bytes 100
  61.6 16.5 %all-to-all-start.2 = ((f32[64,8,6]{2,1,0:T(8,128)}), f32[64,8,6]{2,1,0:T(8,128)S(1)}, u32[]{:S(2)}, u32[]{:S(2)}) async-start(f32[64,8,6]{2,1,0:T(8,128)} %broadcast_in_dim.49), calls=%async_computation.2 | async-start | bytes 524288 | tf_op jit(solution)/shard_map/all_to_all | solution.py:13
  67.6 15.4 %copy-start.13 = (bf16[2,3,2,64]{3,2,1,0:T(2,128)(2,1)S(1)}, bf16[2,3,2,64]{3,2,1,0:T(2,128)(2,1)}, u32[]{:S(2)}) copy-start(bf16[2,3,2,64]{3,2,1,0:T(2,128)(2,1)} %param.36) | copy-start | bytes 4612
  67.6 16.0 %copy-start.17 = (s32[16]{0:T(128)S(1)}, s32[16]{0:T(128)}, u32[]{:S(2)}) copy-start(s32[16]{0:T(128)} %param.20) | copy-start | bytes 196
  67.6 16.6 %copy-start.18 = (f32[2]{0:T(128)S(1)}, f32[2]{0:T(128)}, u32[]{:S(2)}) copy-start(f32[2]{0:T(128)} %param.30) | copy-start | bytes 28
  78.1 28.5 %all-to-all-start.4 = ((bf16[16,2,2,64,128]{4,3,2,1,0:T(8,128)(2,1)}), bf16[16,2,2,64,128]{4,3,2,1,0:T(8,128)(2,1)S(1)}, u32[]{:S(2)}, u32[]{:S(2)}) async-start(bf16[16,2,2,64,128]{4,3,2,1,0:T(8,128)(2,1)} %copy.227), calls=%async_computation.4 | async-start | bytes 2097152 | tf_op jit(solution)/shard_map/all_to_all | solution.py:45
  86.3 20.5 %copy-start.10 = (bf16[2,384]{1,0:T(2,128)(2,1)S(1)}, bf16[2,384]{1,0:T(2,128)(2,1)}, u32[]{:S(2)}) copy-start(bf16[2,384]{1,0:T(2,128)(2,1)} %reshape.389) | copy-start | bytes 4612
  86.3 20.5 %copy-start.14 = (bf16[2,3,256]{2,0,1:T(2,128)(2,1)S(1)}, bf16[2,3,256]{2,0,1:T(2,128)(2,1)}, u32[]{:S(2)}) copy-start(bf16[2,3,256]{2,0,1:T(2,128)(2,1)} %param.37) | copy-start | bytes 9220
  93.2 34.4 %copy-start.19 = (s32[2]{0:T(128)S(1)}, s32[2]{0:T(128)}, u32[]{:S(2)}) copy-start(s32[2]{0:T(128)} %dynamic_slice.7) | copy-start | bytes 28
  93.2 34.8 %copy-start.5 = (f32[2,1,2,64]{3,0,2,1:T(2,128)S(1)}, f32[2,1,2,64]{3,0,2,1:T(2,128)}, u32[]{:S(2)}) copy-start(f32[2,1,2,64]{3,0,2,1:T(2,128)} %get-tuple-element.51) | copy-start | bytes 3076
  93.2 34.8 %copy-start.12 = (f32[4,2,64]{2,1,0:T(2,128)S(1)}, f32[4,2,64]{2,1,0:T(2,128)}, u32[]{:S(2)}) copy-start(f32[4,2,64]{2,1,0:T(2,128)} %param.25) | copy-start | bytes 6148
  93.2 34.8 %copy-start.15 = (f32[2,64]{1,0:T(2,128)S(1)}, f32[2,64]{1,0:T(2,128)}, u32[]{:S(2)}) copy-start(f32[2,64]{1,0:T(2,128)} %param.26) | copy-start | bytes 1540
  130.8 2.4 %copy-start.6 = (f32[2,2,64]{2,0,1:T(2,128)S(1)}, f32[2,2,64]{2,0,1:T(2,128)}, u32[]{:S(2)}) copy-start(f32[2,2,64]{2,0,1:T(2,128)} %get-tuple-element.44) | copy-start | bytes 3076
  130.8 2.4 %copy-start.7 = (f32[2,2,64]{2,0,1:T(2,128)S(1)}, f32[2,2,64]{2,0,1:T(2,128)}, u32[]{:S(2)}) copy-start(f32[2,2,64]{2,0,1:T(2,128)} %get-tuple-element.76) | copy-start | bytes 3076
  130.8 2.4 %copy-start.8 = (f32[2,2,64]{2,0,1:T(2,128)S(1)}, f32[2,2,64]{2,0,1:T(2,128)}, u32[]{:S(2)}) copy-start(f32[2,2,64]{2,0,1:T(2,128)} %get-tuple-element.78) | copy-start | bytes 3076
  130.8 2.4 %copy-start.9 = (f32[2,2,64]{2,0,1:T(2,128)S(1)}, f32[2,2,64]{2,0,1:T(2,128)}, u32[]{:S(2)}) copy-start(f32[2,2,64]{2,0,1:T(2,128)} %get-tuple-element.80) | copy-start | bytes 3076
  130.8 2.4 %copy-start.16 = (f32[2]{0:T(128)S(1)}, f32[2]{0:T(128)}, u32[]{:S(2)}) copy-start(f32[2]{0:T(128)} %param.31) | copy-start | bytes 28
  130.8 30.0 %copy-start.1 = (bf16[2,64,4096]{2,1,0:T(8,128)(2,1)S(1)}, bf16[2,64,4096]{2,1,0:T(8,128)(2,1)}, u32[]{:S(2)}) copy-start(bf16[2,64,4096]{2,1,0:T(8,128)(2,1)} %param.33) | copy-start | bytes 3145732
  132.5 45.1 %copy-start.2 = (f32[2,2,64,128]{3,2,1,0:T(8,128)}, f32[2,2,64,128]{3,2,1,0:T(8,128)S(1)}, u32[]{:S(2)}) copy-start(f32[2,2,64,128]{3,2,1,0:T(8,128)S(1)} %copy.256) | copy-start | bytes 393220
where the time goes:
time: 179 us; the launch traced here: 178 us
  blocking collectives  60.8 us (34%)
  starting transfers between devices  40.8 us (23%)
  waiting for transfers between devices  40 us (22%)
  local copies, waits for them, and re-layouts  21.1 us (12%)
  other arithmetic  9.52 us (5%)
  matrix products  4.86 us (3%)
    all_to_all x3, starting transfers between devices, from_everyone(): lax.all_to_all(jnp.broadcast_to(shard[None], (count, *shard.shape)), axis...  29.2 us
    all_to_all x1, blocking collectives, from_everyone(): lax.all_to_all(jnp.broadcast_to(shard[None], (count, *shard.shape)), axis...  26.3 us
    all_gather x1, blocking collectives, rows_first(): filled = lax.all_gather(both, axis, axis=0, tiled=True)  20.3 us
    all_to_all x3, waiting for transfers between devices, from_everyone(): lax.all_to_all(jnp.broadcast_to(shard[None], (count, *shard.shape)), axis...  20.2 us
    all_to_all x2, waiting for transfers between devices, sum_at_owner(): pieces = lax.all_to_all(split_up(shard, dim, count), axis, 0, 0, tiled=True)  19.8 us
    all_to_all x1, blocking collectives, sum_at_owner_2(): lax.all_to_all(pieces, axis, split_axis=0, concat_axis=0, tiled=True)  14.2 us
    all_to_all x2, starting transfers between devices, sum_at_owner(): pieces = lax.all_to_all(split_up(shard, dim, count), axis, 0, 0, tiled=True)  11.6 us
    unnamed x53, local copies, waits for them, and re-layouts  5.79 us
  transfers between devices with their start and end apart: 5, of which 5 were waited for; matrix products, arithmetic and copies ran while one was open for 12% of the time, Pallas kernels for 0%

commit v1 on v0

--- a/solution.py
+++ b/solution.py
@@ -50,7 +50,9 @@
     turned = [jnp.moveaxis(a, dim, 0) for a, dim in zip(arrays, dims)]
     widths = [t[0].size for t in turned]
     both = jnp.concatenate([t.reshape(-1, w) for t, w in zip(turned, widths)], axis=1)
-    filled = lax.all_gather(both, axis, axis=0, tiled=True)
+    filled = jnp.concatenate(
+        lax.all_to_all(jnp.stack([both] * lax.axis_size(axis)), axis, 0, 0), axis=0
+    )
     pieces = jnp.split(filled, [sum(widths[:k]) for k in range(1, len(widths))], axis=1)
     return tuple(
         (

time: 179 us -> 177 us (0.989)
  blocking collectives: 60.8 us -> 29.9 us
  waiting for transfers between devices: 40 us -> 65.8 us
  starting transfers between devices: 40.8 us -> 43.9 us
  other arithmetic: 9.52 us -> 7.71 us
    all_gather x1 -> x0, blocking collectives: 20.3 us -> none  [rows_first(): filled = lax.all_gather(both, axis, axis=0, tiled=True)]
    all_to_all x2, waiting for transfers between devices: 19.8 us -> 33.1 us  [sum_at_owner(): pieces = lax.all_to_all(split_up(shard, dim, count), axis, 0, 0, tiled=True)]
    all_to_all x0 -> x1, waiting for transfers between devices: none -> 13 us  [rows_first(): lax.all_to_all(jnp.stack([both] * lax.axis_size(axis)), axis, 0, 0)]
    all_to_all x1, blocking collectives: 26.3 us -> 15.6 us  [from_everyone(): lax.all_to_all(jnp.broadcast_to(shard[None], (count, *shard.shape)), axis...]
    all_to_all x0 -> x1, starting transfers between devices: none -> 3.67 us  [rows_first(): lax.all_to_all(jnp.stack([both] * lax.axis_size(axis)), axis, 0, 0)]
    unnamed x53 -> x50, local copies, waits for them, and re-layouts: 5.79 us -> 6.38 us
  transfers between devices with their start and end apart: 5 -> 6, of which waited for: 5 -> 6; matrix products, arithmetic and copies ran while one was open for 12% -> 11% of each run, Pallas kernels for 0% -> 0%
where the time goes in v1:
time: 177 us; the launch traced here: 176 us
  waiting for transfers between devices  65.8 us (37%)
  starting transfers between devices  43.9 us (25%)
  blocking collectives  29.9 us (17%)
  local copies, waits for them, and re-layouts  21.2 us (12%)
  other arithmetic  7.71 us (4%)
  matrix products  6.19 us (3%)
    all_to_all x2, waiting for transfers between devices, sum_at_owner(): pieces = lax.all_to_all(split_up(shard, dim, count), axis, 0, 0, tiled=True)  33.1 us
    all_to_all x3, starting transfers between devices, from_everyone(): lax.all_to_all(jnp.broadcast_to(shard[None], (count, *shard.shape)), axis...  29.8 us
    all_to_all x3, waiting for transfers between devices, from_everyone(): lax.all_to_all(jnp.broadcast_to(shard[None], (count, *shard.shape)), axis...  19.8 us
    all_to_all x1, blocking collectives, from_everyone(): lax.all_to_all(jnp.broadcast_to(shard[None], (count, *shard.shape)), axis...  15.6 us
    all_to_all x1, blocking collectives, sum_at_owner_2(): lax.all_to_all(pieces, axis, split_axis=0, concat_axis=0, tiled=True)  14.2 us
    all_to_all x1, waiting for transfers between devices, rows_first(): lax.all_to_all(jnp.stack([both] * lax.axis_size(axis)), axis, 0, 0)  13 us
    all_to_all x2, starting transfers between devices, sum_at_owner(): pieces = lax.all_to_all(split_up(shard, dim, count), axis, 0, 0, tiled=True)  10.5 us
    unnamed x50, local copies, waits for them, and re-layouts  6.38 us
  transfers between devices with their start and end apart: 6, of which 6 were waited for; matrix products, arithmetic and copies ran while one was open for 11% of the time, Pallas kernels for 0%

profile of v1, /device:TPU:1, one launch (start us, length us, event | category | flops | bytes accessed | tf_op | source)
XLA Modules:
  0.0 176.0 jit_solution(3919949579159300642)
XLA Ops:
  0.7 1.4 broadcast_in_dim.52
  2.1 13.4 %all-to-all-start.3 = ((f32[16,1,2,32]{3,2,1,0:T(2,128)}), f32[16,1,2,32]{3,2,1,0:T(2,128)S(1)}, u32[]{:S(2)}, u32[]{:S(2)}) async-start(f32[16,1,2,32]{3,2,1,0:T(2,128)} %broadcast_in_dim.52), calls=%async_computation.3 | async-start | bytes 32768 | tf_op jit(solution)/shard_map/all_to_all | solution.py:13
  15.5 0.7 fusion.42
  16.3 0.8 multiply_reduce_fusion
  17.2 0.1 copy.217
  17.5 2.5 %copy.218 = bf16[6285,64]{1,0:T(8,128)(2,1)} copy(bf16[6285,64]{0,1:T(8,128)(2,1)} %param.21) | data formatting | bytes 1608960 | tf_op args[2]
  20.1 2.2 %gather_fusion = bf16[64,64]{1,0:T(8,128)(2,1)S(1)} fusion(bf16[6285,64]{1,0:T(8,128)(2,1)} %copy.218, s32[1024]{0:T(1024)S(1)} %pad_clamp_fusion), kind=kCustom, calls=%fused_computation | custom fusion | bytes 16640 | tf_op jit(solution)/shard_map/jit(_take)/gather | solution.py:156
  22.3 0.1 fusion.19
  22.5 0.7 reshape.443
  23.2 1.2 all-to-all-done.3
  24.4 6.8 %all-to-all-start = ((bf16[8,2,256]{2,1,0:T(2,128)(2,1)}), bf16[8,2,256]{2,1,0:T(2,128)(2,1)S(1)}, u32[]{:S(2)}, u32[]{:S(2)}) async-start(bf16[8,2,256]{2,1,0:T(2,128)(2,1)} %reshape.443), calls=%async_computation | async-start | bytes 16384 | tf_op jit(solution)/shard_map/all_to_all | solution.py:45
  31.4 6.3 %all-to-all-done = bf16[8,2,256]{2,1,0:T(2,128)(2,1)S(1)} async-done(((bf16[8,2,256]{2,1,0:T(2,128)(2,1)}), bf16[8,2,256]{2,1,0:T(2,128)(2,1)S(1)}, u32[]{:S(2)}, u32[]{:S(2)}) %all-to-all-start) | async-done | bytes 8224 | tf_op jit(solution)/shard_map/all_to_all | solution.py:45
  38.0 0.8 reshape.445
  38.8 11.3 %all-to-all-start.1 = ((bf16[64,2,256]{2,1,0:T(2,128)(2,1)}), bf16[64,2,256]{2,1,0:T(2,128)(2,1)S(1)}, u32[]{:S(2)}, u32[]{:S(2)}) async-start(bf16[64,2,256]{2,1,0:T(2,128)(2,1)} %reshape.445), calls=%async_computation.1 | async-start | bytes 131072 | tf_op jit(solution)/shard_map/all_to_all | solution.py:13
  50.0 0.3 fusion.2
  50.3 1.1 copy.223
  51.5 8.4 %all-to-all-done.1 = bf16[64,2,256]{2,1,0:T(2,128)(2,1)S(1)} async-done(((bf16[64,2,256]{2,1,0:T(2,128)(2,1)}), bf16[64,2,256]{2,1,0:T(2,128)(2,1)S(1)}, u32[]{:S(2)}, u32[]{:S(2)}) %all-to-all-start.1) | async-done | bytes 65568 | tf_op jit(solution)/shard_map/all_to_all | solution.py:13
  59.8 3.7 %all-to-all-start.4 = ((bf16[16,2,2,64,128]{4,3,2,1,0:T(8,128)(2,1)}), bf16[16,2,2,64,128]{4,3,2,1,0:T(8,128)(2,1)S(1)}, u32[]{:S(2)}, u32[]{:S(2)}) async-start(bf16[16,2,2,64,128]{4,3,2,1,0:T(8,128)(2,1)} %copy.223), calls=%async_computation.4 | async-start | bytes 2097152 | tf_op jit(solution)/shard_map/all_to_all | solution.py:45
  63.6 0.1 reshape.446
  63.8 0.8 copy.220
  64.6 1.1 reshape.402
  65.7 0.3 fusion.5
  66.1 0.2 fusion.86
  66.3 26.7 %all-to-all-done.4 = bf16[16,2,2,64,128]{4,3,2,1,0:T(8,128)(2,1)S(1)} async-done(((bf16[16,2,2,64,128]{4,3,2,1,0:T(8,128)(2,1)}), bf16[16,2,2,64,128]{4,3,2,1,0:T(8,128)(2,1)S(1)}, u32[]{:S(2)}, u32[]{:S(2)}) %all-to-all-start.4) | async-done | bytes 1048608 | tf_op jit(solution)/shard_map/all_to_all | solution.py:45
  93.0 0.7 broadcast_in_dim.49
  93.7 5.1 %all-to-all-start.2 = ((f32[64,8,6]{2,1,0:T(8,128)}), f32[64,8,6]{2,1,0:T(8,128)S(1)}, u32[]{:S(2)}, u32[]{:S(2)}) async-start(f32[64,8,6]{2,1,0:T(8,128)} %broadcast_in_dim.49), calls=%async_computation.2 | async-start | bytes 524288 | tf_op jit(solution)/shard_map/all_to_all | solution.py:13
  98.8 0.8 reduce_sum.72
  99.7 0.9 copy.366
  100.7 10.2 %all-to-all-done.2 = f32[64,8,6]{2,1,0:T(8,128)S(1)} async-done(((f32[64,8,6]{2,1,0:T(8,128)}), f32[64,8,6]{2,1,0:T(8,128)S(1)}, u32[]{:S(2)}, u32[]{:S(2)}) %all-to-all-start.2) | async-done | bytes 12320 | tf_op jit(solution)/shard_map/all_to_all | solution.py:13
  110.9 1.1 stack.12
  112.0 3.7 %all-to-all-start.5 = ((bf16[8,2,17536]{2,1,0:T(2,128)(2,1)}), bf16[8,2,17536]{2,1,0:T(2,128)(2,1)S(1)}, u32[]{:S(2)}, u32[]{:S(2)}) async-start(bf16[8,2,17536]{2,1,0:T(2,128)(2,1)} %stack.12), calls=%async_computation.5 | async-start | bytes 1122304 | tf_op jit(solution)/shard_map/all_to_all | solution.py:54
  115.7 0.7 dynamic_slice.7
  116.3 1.6 fusion.12
  118.1 0.2 reshape_reshape.4
  118.3 0.1 multiply_exponential_fusion.3
  118.8 0.6 copy.241
  119.4 0.6 copy.236
  120.0 0.7 copy.231
  120.7 0.7 copy.222
  121.4 13.0 %all-to-all-done.5 = bf16[8,2,17536]{2,1,0:T(2,128)(2,1)S(1)} async-done(((bf16[8,2,17536]{2,1,0:T(2,128)(2,1)}), bf16[8,2,17536]{2,1,0:T(2,128)(2,1)S(1)}, u32[]{:S(2)}, u32[]{:S(2)}) %all-to-all-start.5) | async-done | bytes 561184 | tf_op jit(solution)/shard_map/all_to_all | solution.py:54
  134.3 0.2 reshape.396
  134.7 0.8 fusion.17
  135.6 0.8 fusion.14
  136.5 1.3 broadcast_multiply_fusion.3
  137.9 0.1 copy.239
  138.0 0.1 copy.234
  138.1 0.1 copy.228
  138.4 0.7 divide_multiply_fusion.10
  139.2 1.7 multiply_add_fusion
  141.0 0.1 fusion.10
  141.1 0.2 fusion.6
  141.3 0.2 fusion.8
  141.4 0.2 fusion.93
  142.0 15.6 %all_to_all.40 = f32[64,4,2]{1,2,0:T(2,128)S(1)} all-to-all(f32[64,4,2]{1,2,0:T(2,128)S(1)} %broadcast_in_dim.54), channel_id=1, replica_groups=mesh['ctx'=16,'dp'=8,'tp'=4] {'ctx','tp'}, dimensions={0} | all-to-all | bytes 4096 | tf_op jit(solution)/shard_map/all_to_all | solution.py:13
  157.8 0.8 multiply_convert_fusion.1
  158.6 0.3 convolution_bitcast_fusion
  158.9 0.2 reshape.401
  159.1 0.2 copy.367
  159.2 0.2 reshape.447
  159.5 14.2 %all_to_all.41 = f32[64,1,512]{2,1,0:T(1,128)S(1)} all-to-all(f32[64,1,512]{2,1,0:T(1,128)S(1)} %reshape.447), channel_id=1, replica_groups=mesh['ctx'=16,'dp'=8,'tp'=4] {'ctx','tp'}, dimensions={0} | all-to-all | bytes 262144 | tf_op jit(solution)/shard_map/all_to_all | solution.py:83
  173.7 0.5 broadcast.322
  174.2 0.9 reduce.20
  175.2 0.2 reshape.448
  175.4 0.6 copy.250
  (95 shorter events, 2.6 us)
Async XLA Ops:
  0.6 115.7 %copy-start = (bf16[2,2,64,4096]{3,2,1,0:T(8,128)(2,1)S(1)}, bf16[2,2,64,4096]{3,2,1,0:T(8,128)(2,1)}, u32[]{:S(2)}) copy-start(bf16[2,2,64,4096]{3,2,1,0:T(8,128)(2,1)} %param.23) | copy-start | bytes 6291460
  0.6 49.4 %copy-start.2 = (bf16[1,2,32,64,128]{4,3,2,1,0:T(8,128)(2,1)S(1)}, bf16[1,2,32,64,128]{4,3,2,1,0:T(8,128)(2,1)}, u32[]{:S(2)}) copy-start(bf16[1,2,32,64,128]{4,3,2,1,0:T(8,128)(2,1)} %param.34) | copy-start | bytes 3145732
  2.1 22.3 %all-to-all-start.3 = ((f32[16,1,2,32]{3,2,1,0:T(2,128)}), f32[16,1,2,32]{3,2,1,0:T(2,128)S(1)}, u32[]{:S(2)}, u32[]{:S(2)}) async-start(f32[16,1,2,32]{3,2,1,0:T(2,128)} %broadcast_in_dim.52), calls=%async_computation.3 | async-start | bytes 32768 | tf_op jit(solution)/shard_map/all_to_all | solution.py:13
  24.4 13.4 %all-to-all-start = ((bf16[8,2,256]{2,1,0:T(2,128)(2,1)}), bf16[8,2,256]{2,1,0:T(2,128)(2,1)S(1)}, u32[]{:S(2)}, u32[]{:S(2)}) async-start(bf16[8,2,256]{2,1,0:T(2,128)(2,1)} %reshape.443), calls=%async_computation | async-start | bytes 16384 | tf_op jit(solution)/shard_map/all_to_all | solution.py:45
  38.8 21.1 %all-to-all-start.1 = ((bf16[64,2,256]{2,1,0:T(2,128)(2,1)}), bf16[64,2,256]{2,1,0:T(2,128)(2,1)S(1)}, u32[]{:S(2)}, u32[]{:S(2)}) async-start(bf16[64,2,256]{2,1,0:T(2,128)(2,1)} %reshape.445), calls=%async_computation.1 | async-start | bytes 131072 | tf_op jit(solution)/shard_map/all_to_all | solution.py:13
  50.3 13.2 %copy-start.13 = (bf16[2,3,2,64]{3,2,1,0:T(2,128)(2,1)S(1)}, bf16[2,3,2,64]{3,2,1,0:T(2,128)(2,1)}, u32[]{:S(2)}) copy-start(bf16[2,3,2,64]{3,2,1,0:T(2,128)(2,1)} %param.36) | copy-start | bytes 4612
  51.4 14.6 %copy-start.4 = (f32[4096]{0:T(1024)S(1)}, f32[4096]{0:T(1024)}, u32[]{:S(2)}) copy-start(f32[4096]{0:T(1024)} %param.22) | copy-start | bytes 49156
  51.5 14.6 %copy-start.5 = (bf16[4096,6]{0,1:T(8,128)(2,1)S(1)}, bf16[4096,6]{0,1:T(8,128)(2,1)}, u32[]{:S(2)}) copy-start(bf16[4096,6]{0,1:T(8,128)(2,1)} %param.24) | copy-start | bytes 147460
  59.8 33.2 %all-to-all-start.4 = ((bf16[16,2,2,64,128]{4,3,2,1,0:T(8,128)(2,1)}), bf16[16,2,2,64,128]{4,3,2,1,0:T(8,128)(2,1)S(1)}, u32[]{:S(2)}, u32[]{:S(2)}) async-start(bf16[16,2,2,64,128]{4,3,2,1,0:T(8,128)(2,1)} %copy.223), calls=%async_computation.4 | async-start | bytes 2097152 | tf_op jit(solution)/shard_map/all_to_all | solution.py:45
  63.5 37.1 %copy-start.14 = (bf16[2,3,256]{2,0,1:T(2,128)(2,1)S(1)}, bf16[2,3,256]{2,0,1:T(2,128)(2,1)}, u32[]{:S(2)}) copy-start(bf16[2,3,256]{2,0,1:T(2,128)(2,1)} %param.37) | copy-start | bytes 9220
  66.0 49.7 %copy-start.18 = (f32[2]{0:T(128)S(1)}, f32[2]{0:T(128)}, u32[]{:S(2)}) copy-start(f32[2]{0:T(128)} %param.30) | copy-start | bytes 28
  66.1 27.7 %copy-start.10 = (f32[8]{0:T(128)}, f32[8]{0:T(128)S(1)}, u32[]{:S(2)}) copy-start(f32[8]{0:T(128)S(1)} %rsqrt.19) | copy-start | bytes 100
  66.1 49.6 %copy-start.16 = (s32[16]{0:T(128)S(1)}, s32[16]{0:T(128)}, u32[]{:S(2)}) copy-start(s32[16]{0:T(128)} %param.20) | copy-start | bytes 196
  93.7 17.1 %all-to-all-start.2 = ((f32[64,8,6]{2,1,0:T(8,128)}), f32[64,8,6]{2,1,0:T(8,128)S(1)}, u32[]{:S(2)}, u32[]{:S(2)}) async-start(f32[64,8,6]{2,1,0:T(8,128)} %broadcast_in_dim.49), calls=%async_computation.2 | async-start | bytes 524288 | tf_op jit(solution)/shard_map/all_to_all | solution.py:13
  112.0 6.3 %copy-start.17 = (f32[2]{0:T(128)S(1)}, f32[2]{0:T(128)}, u32[]{:S(2)}) copy-start(f32[2]{0:T(128)} %param.29) | copy-start | bytes 28
  112.0 22.4 %all-to-all-start.5 = ((bf16[8,2,17536]{2,1,0:T(2,128)(2,1)}), bf16[8,2,17536]{2,1,0:T(2,128)(2,1)S(1)}, u32[]{:S(2)}, u32[]{:S(2)}) async-start(bf16[8,2,17536]{2,1,0:T(2,128)(2,1)} %stack.12), calls=%async_computation.5 | async-start | bytes 1122304 | tf_op jit(solution)/shard_map/all_to_all | solution.py:54
  118.0 18.5 %copy-start.11 = (f32[4,2,64]{2,1,0:T(2,128)S(1)}, f32[4,2,64]{2,1,0:T(2,128)}, u32[]{:S(2)}) copy-start(f32[4,2,64]{2,1,0:T(2,128)} %param.25) | copy-start | bytes 6148
  118.1 20.3 %copy-start.12 = (f32[4,256]{1,0:T(4,128)S(1)}, f32[4,256]{1,0:T(4,128)}, u32[]{:S(2)}) copy-start(f32[4,256]{1,0:T(4,128)} %param.27) | copy-start | bytes 12292
  139.2 2.4 %copy-start.6 = (f32[2,2,64]{2,0,1:T(2,128)S(1)}, f32[2,2,64]{2,0,1:T(2,128)}, u32[]{:S(2)}) copy-start(f32[2,2,64]{2,0,1:T(2,128)} %get-tuple-element.44) | copy-start | bytes 3076
  139.2 2.4 %copy-start.7 = (f32[2,2,64]{2,0,1:T(2,128)S(1)}, f32[2,2,64]{2,0,1:T(2,128)}, u32[]{:S(2)}) copy-start(f32[2,2,64]{2,0,1:T(2,128)} %get-tuple-element.76) | copy-start | bytes 3076
  139.2 2.4 %copy-start.8 = (f32[2,2,64]{2,0,1:T(2,128)S(1)}, f32[2,2,64]{2,0,1:T(2,128)}, u32[]{:S(2)}) copy-start(f32[2,2,64]{2,0,1:T(2,128)} %get-tuple-element.78) | copy-start | bytes 3076
  139.2 2.4 %copy-start.9 = (f32[2,2,64]{2,0,1:T(2,128)S(1)}, f32[2,2,64]{2,0,1:T(2,128)}, u32[]{:S(2)}) copy-start(f32[2,2,64]{2,0,1:T(2,128)} %get-tuple-element.80) | copy-start | bytes 3076
  139.2 2.4 %copy-start.15 = (f32[2]{0:T(128)S(1)}, f32[2]{0:T(128)}, u32[]{:S(2)}) copy-start(f32[2]{0:T(128)} %param.31) | copy-start | bytes 28
  139.2 19.3 %copy-start.1 = (bf16[2,64,4096]{2,1,0:T(8,128)(2,1)S(1)}, bf16[2,64,4096]{2,1,0:T(8,128)(2,1)}, u32[]{:S(2)}) copy-start(bf16[2,64,4096]{2,1,0:T(8,128)(2,1)} %param.33) | copy-start | bytes 3145732
  141.0 34.5 %copy-start.3 = (f32[2,2,64,128]{3,2,1,0:T(8,128)}, f32[2,2,64,128]{3,2,1,0:T(8,128)S(1)}, u32[]{:S(2)}) copy-start(f32[2,2,64,128]{3,2,1,0:T(8,128)S(1)} %copy.251) | copy-start | bytes 393220
